TPU v7x, 32 devices: a whole 2x2x4 slice. The times are simulated.
32 devices in a mesh: width: 4 (over y, x), store: 8 (over z, core).
Axes of the slice: x: 2, y: 2, z: 4, core: 2. Of those that a mesh axis runs over, the one named last changes fastest.
Arguments:
- activations: bfloat16 [64, 512, 8192], P('store', None, 'width'), may hold values from -6 to 6
- out_grads: bfloat16 [64, 512, 8192], P('store', None, 'width'), may hold values from -6 to 6
- proj_in: bfloat16 [8192, 64], P('width'), may hold values from -0.0625 to 0.0625
- proj_out: bfloat16 [8192, 64], P('width'), may hold values from -0.0625 to 0.0625
- fisher_inv: float32 [4096, 4096], P('store', 'width'), may hold values from -0.09375 to 0.09375
- grad_store: float32 [16384, 4096], P('store', 'width'), may hold values from -6 to 6
Outputs:
- scores: float32 [64, 16384], P('width', 'store')
All inputs are finite; a program needn't handle non-finite values.
Results may differ from a plain program's by a relative error of at most 0.0003.
Values sent between devices are 32-bit elements; how exact they have to be, the bound alone decides.
A program may use at most 128 MiB of HBM per device.

v0:
```python
import jax
import jax.numpy as jnp
from jax import lax
from jax.sharding import PartitionSpec as P

RANK = 64
SEQ = 512
COORD = 4096


def outer_mean(paired):
    grad_side = paired[:, :, :RANK]
    act_side = paired[:, :, RANK:]
    result = jnp.einsum("qti,qtj->qij", grad_side, act_side, precision=lax.Precision.HIGHEST) / SEQ
    return result.reshape(paired.shape[0], COORD)


def body(activations, out_grads, proj_in, proj_out, fisher_inv, grad_store):
    act_proj = jnp.einsum("qtd,dr->qtr", activations, proj_in, preferred_element_type=jnp.float32)
    grad_proj = jnp.einsum("qtd,dr->qtr", out_grads, proj_out, preferred_element_type=jnp.float32)
    paired = jnp.concatenate([grad_proj, act_proj], axis=2)
    summed = lax.psum(paired, "width")
    gradient = outer_mean(summed)
    blocks = lax.all_to_all(gradient, "store", split_axis=1, concat_axis=0, tiled=True)
    partial_sum = jnp.dot(blocks, fisher_inv, precision=lax.Precision.HIGHEST)
    precond = lax.psum(partial_sum, "store")
    return lax.psum_scatter(
        jnp.dot(precond, grad_store.T, precision=lax.Precision.HIGHEST),
        "width",
        scatter_dimension=0,
        tiled=True,
    )


def solution(mesh):
    placed = (
        P("store", None, "width"),
        P("store", None, "width"),
        P("width", None),
        P("width", None),
        P("store", "width"),
        P("store", "width"),
    )
    return jax.shard_map(
        body, mesh=mesh, in_specs=placed, out_specs=P("width", "store"), check_vma=False
    )
```

profile of v0, /device:TPU:0, one launch (start us, length us, event | category | flops | bytes accessed | tf_op | source)
XLA Modules:
  0.0 208.8 jit_solution(8943537530156808582)
XLA Ops:
  6.5 0.0 copy-start
  6.5 0.0 copy-start.2
  6.5 0.0 all-reduce.3.cloned.1.call-start
  6.5 0.0 copy-start.1
  6.5 11.1 %fusion.2 = f32[8,512,64]{1,2,0:T(8,128)S(1)} fusion(bf16[8,512,2048]{2,1,0:T(8,128)(2,1)} %param.6, bf16[2048,64]{0,1:T(8,128)(2,1)} %param.8), kind=kOutput, calls=%fused_computation.4 | convolution fusion | flops 1073741824 | bytes 18087936 | tf_op jit(solution)/shard_map/qtd,dr->qtr/dot_general | solution.py:19
  17.6 0.0 copy-done.2
  17.6 0.0 copy-done.1
  17.7 5.2 %fusion.4 = f32[8,512,64]{1,2,0:T(8,128)S(1)} fusion(bf16[8,512,2048]{2,1,0:T(8,128)(2,1)S(1)} %copy-done.1, bf16[2048,64]{0,1:T(8,128)(2,1)S(1)} %copy-done.2), kind=kOutput, calls=%fused_computation.6 | convolution fusion | flops 1073741824 | bytes 18087936 | tf_op jit(solution)/shard_map/qtd,dr->qtr/dot_general | solution.py:20
  22.8 1.5 pad_maximum_fusion
  24.3 0.0 all-reduce.3.cloned.1.call-update
  24.3 0.0 all-reduce.5.cloned.1.call-start
  24.4 72.5 %all-reduce.3.cloned.1.call-done = f32[8,512,128]{1,2,0:T(8,128)} async-done(((f32[8,512,128]{1,2,0:T(8,128)}), f32[8,512,128]{1,2,0:T(8,128)}) %all-reduce.3.cloned.1.call-update) | async-done | bytes 2097168 | tf_op jit(solution)/shard_map/psum | solution.py:22
  96.9 2.6 %convolution_multiply_fusion = f32[8,64,64]{2,1,0:T(8,128)S(1)} fusion(f32[8,512,128]{1,2,0:T(8,128)} %all-reduce.3.cloned.1.call-done), kind=kOutput, calls=%fused_computation.1 | convolution fusion | flops 201359360 | bytes 2228224 | tf_op jit(solution)/shard_map/qti,qtj->qij/dot_general | solution.py:14
  99.5 0.1 all_to_all.14
  99.6 0.1 copy.7
  99.7 11.2 %all_to_all.19 = f32[8,8,512]{2,0,1:T(8,128)S(1)} all-to-all(f32[8,8,512]{2,0,1:T(8,128)S(1)} %copy.7), channel_id=1, replica_groups=mesh['width'=4,'store'=8] {'store'}, dimensions={1} | all-to-all | bytes 262144 | tf_op jit(solution)/shard_map/all_to_all | solution.py:24
  110.9 0.0 copy-done
  110.9 2.1 fusion.6
  113.0 0.0 all-reduce.5.cloned.1.call-update
  113.0 0.2 reduce-scatter.2.cloned.1.call-start
  113.2 52.9 %all-reduce.5.cloned.1.call-done = f32[64,1024]{1,0:T(8,128)} async-done(((f32[64,1024]{1,0:T(8,128)}), f32[64,1024]{1,0:T(8,128)}) %all-reduce.5.cloned.1.call-update) | async-done | bytes 262160 | tf_op jit(solution)/shard_map/psum | solution.py:26
  166.1 12.2 %fusion.8 = f32[64,2048]{1,0:T(8,128)} fusion(f32[64,1024]{1,0:T(8,128)} %all-reduce.5.cloned.1.call-done, f32[2048,1024]{1,0:T(8,128)} %param.11), kind=kOutput, calls=%fused_computation.10 | convolution fusion | flops 1610612736 | bytes 9175040 | tf_op jit(solution)/shard_map/dot_general | solution.py:28
  178.4 0.0 reduce-scatter.2.cloned.1.call-update
  178.4 23.9 %reduce-scatter.2.cloned.1.call-done = f32[16,2048]{1,0:T(8,128)} async-done(((f32[64,2048]{1,0:T(8,128)}), f32[16,2048]{1,0:T(8,128)}) %reduce-scatter.2.cloned.1.call-update) | async-done | bytes 131088 | tf_op jit(solution)/shard_map/reduce_scatter | solution.py:27
Async XLA Ops:
  6.5 104.3 %copy-start = (f32[512,1024]{1,0:T(8,128)S(1)}, f32[512,1024]{1,0:T(8,128)}, u32[]{:S(2)}) copy-start(f32[512,1024]{1,0:T(8,128)} %param.10) | copy-start | bytes 6291460
  6.5 11.1 %copy-start.2 = (bf16[2048,64]{0,1:T(8,128)(2,1)S(1)}, bf16[2048,64]{0,1:T(8,128)(2,1)}, u32[]{:S(2)}) copy-start(bf16[2048,64]{0,1:T(8,128)(2,1)} %param.9) | copy-start | bytes 786436
  6.5 90.3 %all-reduce.3.cloned.1.call-start = ((), (), s32[]{:S(2)}) async-start(), calls=%async_computation.2 | async-start | bytes 4194304 | tf_op jit(solution)/shard_map/psum | solution.py:22
  6.5 11.1 %copy-start.1 = (bf16[8,512,2048]{2,1,0:T(8,128)(2,1)S(1)}, bf16[8,512,2048]{2,1,0:T(8,128)(2,1)}, u32[]{:S(2)}) copy-start(bf16[8,512,2048]{2,1,0:T(8,128)(2,1)} %param.7) | copy-start | bytes 50331652
  24.3 141.8 %all-reduce.5.cloned.1.call-start = ((), (), s32[]{:S(2)}) async-start(), calls=%async_computation.3 | async-start | bytes 524288 | tf_op jit(solution)/shard_map/psum | solution.py:26
  113.0 89.3 %reduce-scatter.2.cloned.1.call-start = ((), (), s32[]{:S(2)}) async-start(), calls=%async_computation.4 | async-start | bytes 655360 | tf_op jit(solution)/shard_map/reduce_scatter | solution.py:27
Sparse Core Ops, SparseCore 0:
  24.5 72.3 all-reduce.2
  113.1 52.9 all-reduce.4
  178.5 23.7 reduce-scatter.1
where the time goes:
time: 209 us
  waiting for transfers between devices  149 us (71%)
  matrix products  33.2 us (16%)
  between operations  13.1 us (6%)
  blocking collectives  11.2 us (5%)
    psum x1, waiting for transfers between devices, body(): summed = lax.psum(paired, 'width')  72.5 us
    psum x1, waiting for transfers between devices, body(): precond = lax.psum(partial_sum, 'store')  52.9 us
    reduce_scatter x1, waiting for transfers between devices, body(): lax.psum_scatter(jnp.dot(precond, grad_store.T, precision=lax.Precision.H...  23.9 us
    dot_general x1, matrix products, body(): jnp.dot(precond, grad_store.T, precision=lax.Precision.HIGHEST)  12.2 us
    all_to_all x1, blocking collectives, body(): lax.all_to_all(gradient, 'store', split_axis=1, concat_axis=0, tiled=True)  11.2 us
    dot_general x1, matrix products, body(): jnp.einsum('qtd,dr->qtr', activations, proj_in, preferred_element_type=jn...  11.1 us
    dot_general x1, matrix products, body(): jnp.einsum('qtd,dr->qtr', out_grads, proj_out, preferred_element_type=jnp...  5.18 us
  transfers between devices with their start and end apart: 3, of which 3 were waited for; matrix products, arithmetic and copies ran while one was open for 0% of the time, Pallas kernels for 0%

commit v1 on v0

v1 whole, which is shorter than its diff:
```python
import functools

import jax
import jax.numpy as jnp
from jax import lax
from jax.experimental import pallas as pl
from jax.experimental.pallas import tpu as pltpu
from jax.sharding import PartitionSpec as P

DEPTH = 4
COLS = 4
LANES = 128
F32, BF16 = jnp.float32, jnp.bfloat16


def split(value):
    high = value.astype(BF16)
    return high, (value - high.astype(F32)).astype(BF16)


def dot(a, b, dims=((1,), (0,))):
    return lax.dot_general(a, b, (dims, ((), ())), preferred_element_type=F32)


def plan(tall, per):
    first_x = [(dy, 1, p, 0) for dy in list(range(1, tall)) + [0] for p in range(per)]
    first_y = [(dy, dx, p, 1) for dx in (1, 0) for dy in range(1, tall) for p in range(per)]
    one = []
    for i in range(max(len(first_x), len(first_y))):
        one += first_x[i : i + 1] + first_y[i : i + 1]
    two = [(dy, 0, p, 0) for dy in range(1, tall) for p in range(per)] + [(0, 1, p, 1) for p in range(per)]
    own = [(0, 0, p, h) for p in range(per) for h in range(2)]
    return one, two, own


def pick(k, values):
    found = jnp.int32(values[0])
    for i, value in enumerate(values[1:]):
        found = jnp.where(k == i + 1, jnp.int32(value), found)
    return found


def kernel(dims, act, grd, pin, pout, fis, sto, out, abuf, gbuf, win, wout, held, recv1, recv2, sraw, shi, slo, fraw,
           fhi, flo, gsend, graw, pp, prs, pred, pfull, scb, rsc, lsem, bsem, s1, r1, s2, r2, sa, ra, sb, rb, sr, rr, sg,
           rg, sc, rc):
    wide, stores, per, seq, rank = dims
    tall, half, count = wide // 2, seq // 2, wide * stores
    w, s = lax.axis_index("width"), lax.axis_index("store")
    y, x = w // 2, w % 2
    one, two, own = plan(tall, per)
    chunks = one + two + own
    place = {c: i for i, c in enumerate(chunks)}
    n1 = len(one)

    def remote(src, dst, send, recv, axis, index):
        return pltpu.make_async_remote_copy(src_ref=src, dst_ref=dst, send_sem=send, recv_sem=recv,
                                            device_id={axis: index}, device_id_type=pl.DeviceIdType.MESH)

    def owner_of(k):
        dy, dx, p, h = (pick(k, [c[i] for c in chunks]) for i in range(4))
        return dy, dx, p, h

    def loads(k):
        dy, dx, p, h = owner_of(k)
        owner = ((y + dy) % tall) * 2 + (x + dx) % 2
        rows = pl.ds(pl.multiple_of((owner * per + p) * seq + h * half, half), half)
        slot = k % DEPTH
        return (pltpu.make_async_copy(grd.at[rows, :], gbuf.at[slot], bsem.at[0, slot]),
                pltpu.make_async_copy(act.at[rows, :], abuf.at[slot], bsem.at[1, slot]))

    for k in range(DEPTH):
        for load in loads(jnp.int32(k)):
            load.start()

    barrier = pltpu.get_barrier_semaphore()
    for axis, me, size in (("width", w, wide), ("store", s, stores)):
        for d in range(1, size):
            pl.semaphore_signal(barrier, inc=1, device_id={axis: (me + d) % size}, device_id_type=pl.DeviceIdType.MESH)

    blank = jnp.zeros(pin.shape, BF16)
    wout[...] = jnp.concatenate([pout[...], blank], axis=1)
    win[...] = jnp.concatenate([blank, pin[...]], axis=1)
    pl.semaphore_wait(barrier, wide + stores - 2)

    def project(k, carry):
        for load in loads(k):
            load.wait()
        slot = k % DEPTH
        held[k] = dot(gbuf[slot], wout[...]) + dot(abuf[slot], win[...])

        @pl.when(k < n1)
        def _():
            dy, dx, p, h = owner_of(k)
            target = ((y + dy * h) % tall) * 2 + (x + 1 - h) % 2
            remote(held.at[k], recv1.at[k], s1.at[k], r1.at[k], "width", target).start()

        @pl.when(k + DEPTH < len(chunks))
        def _():
            for load in loads(k + DEPTH):
                load.start()

        return carry

    lax.fori_loop(0, len(chunks), project, 0)

    load_f = pltpu.make_async_copy(fis, fraw, lsem.at[0])
    load_s = pltpu.make_async_copy(sto, sraw, lsem.at[1])
    load_f.start()
    load_s.start()

    def got1(c):
        k = place[c]
        remote(held.at[k], recv1.at[k], s1.at[k], r1.at[k], "width", w).wait_recv()
        return recv1[k]

    def got2(c):
        k = place[c] - n1
        remote(held.at[k + n1], recv2.at[k], s2.at[k], r2.at[k], "width", w).wait_recv()
        return recv2[k]

    for c in two:
        dy, dx, p, h = c
        k = place[c]
        total = held[k]
        for other in ([(dy, 1, p, 0)] if h == 0 else [(e, 1, p, 1) for e in range(1, tall)]):
            total = total + got1(other)
        held[k] = total
        target = ((y + dy) % tall) * 2 + (x + dx) % 2
        remote(held.at[k], recv2.at[k - n1], s2.at[k - n1], r2.at[k - n1], "width", target).start()

    load_f.wait()
    fhi[...], flo[...] = split(fraw[...])
    load_s.wait()
    step = sto.shape[0] // 16

    def split_store(i, carry):
        rows = pl.ds(pl.multiple_of(i * step, step), step)
        shi[rows, :], slo[rows, :] = split(sraw[rows, :])
        return carry

    lax.fori_loop(0, 16, split_store, 0)

    lane = lax.broadcasted_iota(jnp.int32, (rank, LANES), 1)
    packed = jnp.zeros((rank, LANES), F32)
    for p in range(per):
        top = held[place[0, 0, p, 0]] + got1((0, 1, p, 0))
        low = held[place[0, 0, p, 1]] + got2((0, 1, p, 1))
        for dy in range(1, tall):
            top = top + got2((dy, 0, p, 0))
            low = low + got1((dy, 0, p, 1))
        both = jnp.concatenate(split(jnp.concatenate([top, low], axis=0)), axis=1)
        outer = dot(both, both, ((0,), (0,)))
        mean = (outer[:rank, :LANES] + outer[:rank, LANES:] + outer[LANES : LANES + rank, :LANES]) * (1.0 / seq)
        if p == 0:
            packed = jnp.where(lane < rank, pltpu.roll(mean, rank, 1), packed)
        else:
            packed = jnp.where(lane >= rank, mean, packed)
    rows_i = rank // stores
    gsend[...] = packed.reshape(stores, rows_i, LANES)

    def ship_a(d):
        peer = (s + d) % stores
        return remote(gsend.at[peer], graw.at[s, w], sa.at[d], ra.at[d], "store", peer)

    for d in range(1, stores):
        ship_a(d).start()
    graw[s, w] = gsend[s]
    for d in range(1, stores):
        ship_a(d).wait_recv()

    def ship_b(d):
        return remote(graw.at[:, w], graw.at[:, w], sb.at[d], rb.at[d], "width", (w + d) % wide)

    for d in range(1, wide):
        ship_b(d).start()
    for d in range(1, wide):
        ship_b(d).wait_recv()

    got = graw[...].reshape(count, rows_i, LANES)
    lane = lax.broadcasted_iota(jnp.int32, (count, LANES), 1)
    sides = [[] for _ in range(per)]
    for i in range(0, rows_i, 2):
        even, odd = got[:, i, :], got[:, i + 1, :]
        sides[0].append(jnp.where(lane < rank, even, pltpu.roll(odd, rank, 1)))
        if per == 2:
            sides[1].append(jnp.where(lane < rank, pltpu.roll(even, rank, 1), odd))
    left = jnp.concatenate([jnp.concatenate(side, axis=1) for side in sides], axis=0)
    queries = per * count
    lhi, llo = split(left)
    two_rows = dot(jnp.concatenate([lhi, llo], axis=0), fhi[...])
    partial = two_rows[:queries] + two_rows[queries:] + dot(lhi, flo[...])
    pp[...] = partial.reshape(pp.shape)

    def ship_r(d):
        peer = (s + d) % stores
        return remote(pp.at[peer], prs.at[d], sr.at[d], rr.at[d], "store", peer)

    for d in range(1, stores):
        ship_r(d).start()
    total = pp[s]
    for d in range(1, stores):
        ship_r(d).wait_recv()
        total = total + prs[d]
    pred[...] = total

    def ship_g(d):
        return remote(pred, pfull.at[s], sg.at[d], rg.at[d], "store", (s + d) % stores)

    for d in range(1, stores):
        ship_g(d).start()
    pfull[s] = total
    for d in range(1, stores):
        ship_g(d).wait_recv()

    precond = pfull[...].reshape(queries, pfull.shape[2])
    phi, plo = split(precond)
    stacked = jnp.concatenate([phi, plo], axis=0)
    span = sto.shape[0] // COLS

    def ship_c(c, d):
        peer = (w + d) % wide
        return remote(scb.at[c, peer], rsc.at[c, d], sc.at[c, d], rc.at[c, d], "width", peer)

    for c in range(COLS):
        rows = pl.ds(c * span, span)
        wide_rows = dot(stacked, shi[rows, :], ((1,), (1,)))
        score = wide_rows[:queries] + wide_rows[queries:] + dot(phi, slo[rows, :], ((1,), (1,)))
        for r in range(wide):
            for p in range(per):
                at = p * count + r * stores
                scb[c, r, p * stores : (p + 1) * stores, :] = score[at : at + stores]
        for d in range(1, wide):
            ship_c(c, d).start()
    for c in range(COLS):
        total = scb[c, w]
        for d in range(1, wide):
            ship_c(c, d).wait_recv()
            total = total + rsc[c, d]
        out[:, c * span : (c + 1) * span] = total

    for k in range(n1):
        remote(held.at[k], recv1.at[k], s1.at[k], r1.at[k], "width", w).wait_send()
    for k in range(len(two)):
        remote(held.at[k + n1], recv2.at[k], s2.at[k], r2.at[k], "width", w).wait_send()
    for d in range(1, stores):
        ship_a(d).wait_send()
        ship_r(d).wait_send()
        ship_g(d).wait_send()
    for d in range(1, wide):
        ship_b(d).wait_send()
        for c in range(COLS):
            ship_c(c, d).wait_send()


def body(wide, stores, activations, out_grads, proj_in, proj_out, fisher_inv, grad_store):
    group, seq, width = activations.shape
    rank = proj_in.shape[1]
    per = group // wide
    half = seq // 2
    one, two, own = plan(wide // 2, per)
    examples, coords = grad_store.shape
    queries = group * stores
    block, out_rows = queries // stores, queries // wide
    rows_i = rank // stores
    span = examples // COLS
    dma = pltpu.SemaphoreType.DMA
    flat = (group * seq, width)
    n1, n2 = len(one), len(two)
    result = pl.pallas_call(
        functools.partial(kernel, (wide, stores, per, seq, rank)),
        out_shape=jax.ShapeDtypeStruct((out_rows, examples), F32),
        in_specs=[pl.BlockSpec(memory_space=pl.ANY)] * 2
        + [pl.BlockSpec(memory_space=pltpu.VMEM)] * 2
        + [pl.BlockSpec(memory_space=pl.ANY)] * 2,
        out_specs=pl.BlockSpec(memory_space=pltpu.VMEM),
        scratch_shapes=[
            pltpu.VMEM((DEPTH, half, width), BF16),
            pltpu.VMEM((DEPTH, half, width), BF16),
            pltpu.VMEM((width, LANES), BF16),
            pltpu.VMEM((width, LANES), BF16),
            pltpu.VMEM((n1 + n2 + len(own), half, LANES), F32),
            pltpu.VMEM((n1, half, LANES), F32),
            pltpu.VMEM((n2, half, LANES), F32),
            pltpu.VMEM(grad_store.shape, F32),
            pltpu.VMEM(grad_store.shape, BF16),
            pltpu.VMEM(grad_store.shape, BF16),
            pltpu.VMEM(fisher_inv.shape, F32),
            pltpu.VMEM(fisher_inv.shape, BF16),
            pltpu.VMEM(fisher_inv.shape, BF16),
            pltpu.VMEM((stores, rows_i, LANES), F32),
            pltpu.VMEM((stores, wide, rows_i, LANES), F32),
            pltpu.VMEM((stores, block, coords), F32),
            pltpu.VMEM((stores, block, coords), F32),
            pltpu.VMEM((block, coords), F32),
            pltpu.VMEM((stores, block, coords), F32),
            pltpu.VMEM((COLS, wide, out_rows, span), F32),
            pltpu.VMEM((COLS, wide, out_rows, span), F32),
            dma((2,)),
            dma((2, DEPTH)),
            dma((n1,)),
            dma((n1,)),
            dma((n2,)),
            dma((n2,)),
            dma((stores,)),
            dma((stores,)),
            dma((wide,)),
            dma((wide,)),
            dma((stores,)),
            dma((stores,)),
            dma((stores,)),
            dma((stores,)),
            dma((COLS, wide)),
            dma((COLS, wide)),
        ],
        compiler_params=pltpu.CompilerParams(collective_id=0, has_side_effects=True, vmem_limit_bytes=56 * 2**20),
        name="influence",
    )(activations.reshape(flat), out_grads.reshape(flat), proj_in, proj_out, fisher_inv, grad_store)
    return result.reshape(per, out_rows // per, examples).transpose(1, 0, 2).reshape(out_rows, examples)


def solution(mesh):
    placed = (
        P("store", None, "width"),
        P("store", None, "width"),
        P("width", None),
        P("width", None),
        P("store", "width"),
        P("store", "width"),
    )
    return jax.shard_map(
        functools.partial(body, mesh.shape["width"], mesh.shape["store"]),
        mesh=mesh, in_specs=placed, out_specs=P("width", "store"), check_vma=False,
    )
```

time: 209 us -> 62.4 us (0.30)
  waiting for transfers between devices: 149 us -> 0 us
  Pallas kernels: 0 us -> 56.5 us
  matrix products: 33.2 us -> 0 us
  between operations: 13.1 us -> 0.01 us
  blocking collectives: 11.2 us -> 0 us
  local copies, waits for them, and re-layouts: 0.21 us -> 5.67 us
    psum x2 -> x0, waiting for transfers between devices: 125 us -> none  [the longest x1 72.5 us: body(): summed = lax.psum(paired, 'width')]
    pallas_call x0 -> x1, Pallas kernels: none -> 56.5 us  [body(): pl.pallas_call(functools.partial(kernel, (wide, stores, per, seq, rank)),...]
    dot_general x5 -> x0, matrix products: 33.2 us -> none  [the longest x1 12.2 us: body(): jnp.dot(precond, grad_store.T, precision=lax.Precision.HIGHEST)]
    reduce_scatter x1 -> x0, waiting for transfers between devices: 23.9 us -> none  [body(): lax.psum_scatter(jnp.dot(precond, grad_store.T, precision=lax.Precision.H...]
    all_to_all x1 -> x0, blocking collectives: 11.2 us -> none  [body(): lax.all_to_all(gradient, 'store', split_axis=1, concat_axis=0, tiled=True)]
    unnamed x6 -> x2, local copies, waits for them, and re-layouts: 0.01 us -> 3.92 us
  transfers between devices with their start and end apart: 3 -> 0, of which waited for: 3 -> 0; matrix products, arithmetic and copies ran while one was open for 0% -> 0% of each run, Pallas kernels for 0% -> 0%
where the time goes in v1:
time: 62.4 us; the launch traced here: 62.2 us
  Pallas kernels  56.5 us (91%)
  local copies, waits for them, and re-layouts  5.67 us (9%)
    pallas_call x1, Pallas kernels, body(): pl.pallas_call(functools.partial(kernel, (wide, stores, per, seq, rank)),...  56.5 us
    unnamed x2, local copies, waits for them, and re-layouts  3.92 us

profile of v1, /device:TPU:0, one launch (start us, length us, event | category | flops | bytes accessed | tf_op | source)
XLA Modules:
  0.0 62.2 jit_solution(14087219976592560265)
XLA Ops:
  0.0 1.9 %copy.7.pin = bf16[2048,64]{1,0:T(8,128)(2,1)} copy(bf16[2048,64]{0,1:T(8,128)(2,1)} %param.8) | data formatting | bytes 524288 | tf_op args[2]
  1.9 2.0 %copy.8.pout = bf16[2048,64]{1,0:T(8,128)(2,1)} copy(bf16[2048,64]{0,1:T(8,128)(2,1)} %param.9) | data formatting | bytes 524288 | tf_op args[3]
  3.9 56.5 %influence.1 = f32[16,2048]{1,0:T(8,128)} custom-call(bf16[4096,2048]{1,0:T(8,128)(2,1)} %bitcast.5, bf16[4096,2048]{1,0:T(8,128)(2,1)} %bitcast.6, bf16[2048,64]{1,0:T(8,128)(2,1)} %copy.7.pin, bf16[2048,64]{1,0:T(8,128)(2,1)} %copy.8.pout, f32[512,1024]{1,0:T(8,128)} %fis.1, f32[2048,1024]{1,0:T(8,128)} %sto.1), custom_call_target="tpu_custom_call" | custom-call | tf_op jit(solution)/shard_map/influence/pallas_call | solution.py:269
  60.4 1.0 %copy.9 = f32[8,2,2048]{2,1,0:T(2,128)S(1)} copy(f32[8,2,2048]{2,0,1:T(8,128)} %bitcast.7) | data formatting | bytes 262144 | tf_op jit(solution)/shard_map/transpose | solution.py:318
  61.4 0.7 %reshape.15 = f32[16,2048]{1,0:T(8,128)} reshape(f32[8,2,2048]{2,1,0:T(2,128)S(1)} %copy.9) | data formatting | bytes 262144 | tf_op jit(solution)/shard_map/reshape | solution.py:318

commit v2 on v0

v2 whole, which is shorter than its diff:
```python
import functools

import jax
import jax.numpy as jnp
from jax import lax
from jax.experimental import pallas as pl
from jax.experimental.pallas import tpu as pltpu
from jax.sharding import PartitionSpec as P

DEPTH = 4
COLS = 4
LANES = 128
F32, BF16 = jnp.float32, jnp.bfloat16


def split(value):
    high = value.astype(BF16)
    return high, (value - high.astype(F32)).astype(BF16)


def dot(a, b, dims=((1,), (0,))):
    return lax.dot_general(a, b, (dims, ((), ())), preferred_element_type=F32)


def plan(tall, p):
    first_x = [(dy, 1, p, 0) for dy in list(range(1, tall)) + [0]]
    first_y = [(dy, dx, p, 1) for dx in (1, 0) for dy in range(1, tall)]
    one = []
    for i in range(max(len(first_x), len(first_y))):
        one += first_x[i : i + 1] + first_y[i : i + 1]
    two = [(dy, 0, p, 0) for dy in range(1, tall)] + [(0, 1, p, 1)]
    own = [(0, 0, p, h) for h in range(2)]
    return one, two, own


def pick(k, values):
    found = jnp.int32(values[0])
    for i, value in enumerate(values[1:]):
        found = jnp.where(k == i + 1, jnp.int32(value), found)
    return found


def kernel(dims, act, grd, pin, pout, fis, sto, out, abuf, gbuf, win, wout, held, recv1, recv2, sraw, shi, slo, fraw,
           fhi, flo, gsend, graw, pp, prs, pred, pfull, scb, rsc, lsem, bsem, s1, r1, s2, r2, sa, ra, sb, rb, sr, rr, sg,
           rg, sc, rc):
    wide, stores, per, seq, rank = dims
    tall, half, count = wide // 2, seq // 2, wide * stores
    w, s = lax.axis_index("width"), lax.axis_index("store")
    y, x = w // 2, w % 2
    plans = [plan(tall, p) for p in range(per)]
    chunks = [c for p in range(per) for group in plans[p] for c in group]
    place = {c: i for i, c in enumerate(chunks)}
    n1, n2 = len(plans[0][0]), len(plans[0][1])
    each = len(chunks) // per

    def remote(src, dst, send, recv, axis, index):
        return pltpu.make_async_remote_copy(src_ref=src, dst_ref=dst, send_sem=send, recv_sem=recv,
                                            device_id={axis: index}, device_id_type=pl.DeviceIdType.MESH)

    def owner_of(k):
        return [pick(k, [c[i] for c in chunks]) for i in range(4)]

    def loads(k):
        dy, dx, p, h = owner_of(k)
        owner = ((y + dy) % tall) * 2 + (x + dx) % 2
        rows = pl.ds(pl.multiple_of((owner * per + p) * seq + h * half, half), half)
        slot = k % DEPTH
        return (pltpu.make_async_copy(grd.at[rows, :], gbuf.at[slot], bsem.at[0, slot]),
                pltpu.make_async_copy(act.at[rows, :], abuf.at[slot], bsem.at[1, slot]))

    for k in range(DEPTH):
        for load in loads(jnp.int32(k)):
            load.start()

    barrier = pltpu.get_barrier_semaphore()
    for axis, me, size in (("width", w, wide), ("store", s, stores)):
        for d in range(1, size):
            pl.semaphore_signal(barrier, inc=1, device_id={axis: (me + d) % size}, device_id_type=pl.DeviceIdType.MESH)

    blank = jnp.zeros(pin.shape, BF16)
    wout[...] = jnp.concatenate([pout[...], blank], axis=0).T
    win[...] = jnp.concatenate([blank, pin[...]], axis=0).T
    pl.semaphore_wait(barrier, wide + stores - 2)

    def project(k, carry):
        for load in loads(k):
            load.wait()
        slot = k % DEPTH
        held[k] = dot(gbuf[slot], wout[...]) + dot(abuf[slot], win[...])

        @pl.when(k % each < n1)
        def _():
            dy, dx, p, h = owner_of(k)
            target = ((y + dy * h) % tall) * 2 + (x + 1 - h) % 2
            at = (k // each) * n1 + k % each
            remote(held.at[k], recv1.at[at], s1.at[at], r1.at[at], "width", target).start()

        @pl.when(k + DEPTH < len(chunks))
        def _():
            for load in loads(k + DEPTH):
                load.start()

        return carry

    def ship_1(c):
        k = place[c]
        at = c[2] * n1 + k % each
        return remote(held.at[k], recv1.at[at], s1.at[at], r1.at[at], "width", w), at

    def ship_2(c):
        k = place[c]
        at = c[2] * n2 + k % each - n1
        target = ((y + c[0]) % tall) * 2 + (x + c[1]) % 2
        return remote(held.at[k], recv2.at[at], s2.at[at], r2.at[at], "width", target), at

    def got1(c):
        copy, at = ship_1(c)
        copy.wait_recv()
        return recv1[at]

    def got2(c):
        copy, at = ship_2(c)
        copy.wait_recv()
        return recv2[at]

    def forward(p):
        for c in plans[p][1]:
            dy, dx, _, h = c
            total = held[place[c]]
            for other in ([(dy, 1, p, 0)] if h == 0 else [(e, 1, p, 1) for e in range(1, tall)]):
                total = total + got1(other)
            held[place[c]] = total
            ship_2(c)[0].start()

    rows_i = rank // stores

    def ship_a(p, d):
        peer = (s + d) % stores
        return remote(gsend.at[p, peer], graw.at[p, s, w], sa.at[p, d], ra.at[p, d], "store", peer)

    def ship_b(p, d):
        return remote(graw.at[p, :, w], graw.at[p, :, w], sb.at[p, d], rb.at[p, d], "width", (w + d) % wide)

    def gradient(p):
        top = held[place[0, 0, p, 0]] + got1((0, 1, p, 0))
        low = held[place[0, 0, p, 1]] + got2((0, 1, p, 1))
        for dy in range(1, tall):
            top = top + got2((dy, 0, p, 0))
            low = low + got1((dy, 0, p, 1))
        both = jnp.concatenate(split(jnp.concatenate([top, low], axis=0)), axis=1)
        outer = dot(both, both, ((0,), (0,)))
        mean = (outer[:rank, :LANES] + outer[:rank, LANES:] + outer[LANES : LANES + rank, :LANES]) * (1.0 / seq)
        gsend[p] = mean.reshape(stores, rows_i, LANES)
        for d in range(1, stores):
            ship_a(p, d).start()
        graw[p, s, w] = gsend[p, s]

    def gather(p):
        for d in range(1, stores):
            ship_a(p, d).wait_recv()
        for d in range(1, wide):
            ship_b(p, d).start()

    by_rows = count % (8 * stores) == 0
    block, coords = pp.shape[2], pp.shape[3]

    def ship_r(p, d):
        peer = (s + d) % stores
        return remote(pp.at[p, peer], prs.at[p, d], sr.at[p, d], rr.at[p, d], "store", peer)

    def ship_g(p, d):
        return remote(pred.at[p], pfull.at[p, s], sg.at[p, d], rg.at[p, d], "store", (s + d) % stores)

    def condition(p):
        for d in range(1, wide):
            ship_b(p, d).wait_recv()
        got = graw[p].reshape(count, rows_i, LANES)
        lane = lax.broadcasted_iota(jnp.int32, (count, LANES), 1)
        pairs = [jnp.where(lane < rank, pltpu.roll(got[:, i, :], rank, 1), got[:, i + 1, :]) for i in range(0, rows_i, 2)]
        left = jnp.concatenate(split(jnp.concatenate(pairs, axis=1)), axis=0)
        double = dot(left, fhi[...]) + dot(left, flo[...])
        partial = double[:count] + double[count:]
        for r in range(stores):
            if by_rows:
                pp[p, r] = partial[r * block : (r + 1) * block]
            else:
                pp[p, r] = partial[:, r * coords : (r + 1) * coords]
        for d in range(1, stores):
            ship_r(p, d).start()

    def combine(p):
        total = pp[p, s]
        for d in range(1, stores):
            ship_r(p, d).wait_recv()
            total = total + prs[p, d]
        pred[p] = total
        pfull[p, s] = total
        for d in range(1, stores):
            ship_g(p, d).start()

    span = sto.shape[0] // COLS

    def ship_c(p, c, d):
        peer = (w + d) % wide
        return remote(scb.at[p, c, peer], rsc.at[p, c, d], sc.at[p, c, d], rc.at[p, c, d], "width", peer)

    def score(p):
        for d in range(1, stores):
            ship_g(p, d).wait_recv()
        precond = jnp.concatenate([pfull[p, r] for r in range(stores)], axis=0 if by_rows else 1)
        stacked = jnp.concatenate(split(precond), axis=0)
        for c in range(COLS):
            rows = pl.ds(c * span, span)
            double = dot(shi[rows, :], stacked, ((1,), (1,))) + dot(slo[rows, :], stacked, ((1,), (1,)))
            double = double.T
            scores = double[:count] + double[count:]
            for r in range(wide):
                scb[p, c, r] = scores[r * stores : (r + 1) * stores]
            for d in range(1, wide):
                ship_c(p, c, d).start()

    def finish(p):
        for c in range(COLS):
            total = scb[p, c, w]
            for d in range(1, wide):
                ship_c(p, c, d).wait_recv()
                total = total + rsc[p, c, d]
            out[p * stores : (p + 1) * stores, c * span : (c + 1) * span] = total

    load_f = pltpu.make_async_copy(fis, fraw, lsem.at[0])
    load_s = pltpu.make_async_copy(sto, sraw, lsem.at[1])

    def split_fisher():
        load_f.wait()
        fhi[...], flo[...] = split(fraw[...])

    def split_store():
        load_s.wait()
        step = sto.shape[0] // 16

        def part(i, carry):
            rows = pl.ds(pl.multiple_of(i * step, step), step)
            shi[rows, :], slo[rows, :] = split(sraw[rows, :])
            return carry

        lax.fori_loop(0, 16, part, 0)

    for p in range(per):
        if p == per - 1:
            load_f.start()
        lax.fori_loop(p * each, (p + 1) * each, project, 0)
        if p + 1 < per:
            forward(p)
    load_s.start()
    split_fisher()
    if per == 2:
        gradient(0)
        gather(0)
        forward(1)
        condition(0)
        split_store()
        gradient(1)
        combine(0)
        gather(1)
        condition(1)
        score(0)
        combine(1)
        score(1)
    else:
        forward(per - 1)
        split_store()
        for p in range(per):
            gradient(p)
            gather(p)
            condition(p)
            combine(p)
            score(p)
    for p in range(per):
        finish(p)

    for p in range(per):
        for c in plans[p][0]:
            ship_1(c)[0].wait_send()
        for c in plans[p][1]:
            ship_2(c)[0].wait_send()
        for d in range(1, stores):
            ship_a(p, d).wait_send()
            ship_r(p, d).wait_send()
            ship_g(p, d).wait_send()
        for d in range(1, wide):
            ship_b(p, d).wait_send()
            for c in range(COLS):
                ship_c(p, c, d).wait_send()


def body(wide, stores, activations, out_grads, proj_in, proj_out, fisher_inv, grad_store):
    group, seq, width = activations.shape
    rank = proj_in.shape[1]
    per = group // wide
    half = seq // 2
    one, two, own = plan(wide // 2, 0)
    n1, n2 = len(one), len(two)
    examples, coords = grad_store.shape
    count = wide * stores
    queries = per * count
    out_rows = queries // wide
    if count % (8 * stores) == 0:
        piece = (count // stores, coords)
    else:
        piece = (count, coords // stores)
    rows_i = rank // stores
    span = examples // COLS
    dma = pltpu.SemaphoreType.DMA
    flat = (group * seq, width)
    result = pl.pallas_call(
        functools.partial(kernel, (wide, stores, per, seq, rank)),
        out_shape=jax.ShapeDtypeStruct((out_rows, examples), F32),
        in_specs=[pl.BlockSpec(memory_space=pl.ANY)] * 2
        + [pl.BlockSpec(memory_space=pltpu.VMEM)] * 2
        + [pl.BlockSpec(memory_space=pl.ANY)] * 2,
        out_specs=pl.BlockSpec(memory_space=pltpu.VMEM),
        scratch_shapes=[
            pltpu.VMEM((DEPTH, half, width), BF16),
            pltpu.VMEM((DEPTH, half, width), BF16),
            pltpu.VMEM((width, LANES), BF16),
            pltpu.VMEM((width, LANES), BF16),
            pltpu.VMEM((per * (n1 + n2 + len(own)), half, LANES), F32),
            pltpu.VMEM((per * n1, half, LANES), F32),
            pltpu.VMEM((per * n2, half, LANES), F32),
            pltpu.VMEM(grad_store.shape, F32),
            pltpu.VMEM(grad_store.shape, BF16),
            pltpu.VMEM(grad_store.shape, BF16),
            pltpu.VMEM(fisher_inv.shape, F32),
            pltpu.VMEM(fisher_inv.shape, BF16),
            pltpu.VMEM(fisher_inv.shape, BF16),
            pltpu.VMEM((per, stores, rows_i, LANES), F32),
            pltpu.VMEM((per, stores, wide, rows_i, LANES), F32),
            pltpu.VMEM((per, stores, *piece), F32),
            pltpu.VMEM((per, stores, *piece), F32),
            pltpu.VMEM((per, *piece), F32),
            pltpu.VMEM((per, stores, *piece), F32),
            pltpu.VMEM((per, COLS, wide, stores, span), F32),
            pltpu.VMEM((per, COLS, wide, stores, span), F32),
            dma((2,)),
            dma((2, DEPTH)),
            dma((per * n1,)),
            dma((per * n1,)),
            dma((per * n2,)),
            dma((per * n2,)),
            dma((per, stores)),
            dma((per, stores)),
            dma((per, wide)),
            dma((per, wide)),
            dma((per, stores)),
            dma((per, stores)),
            dma((per, stores)),
            dma((per, stores)),
            dma((per, COLS, wide)),
            dma((per, COLS, wide)),
        ],
        compiler_params=pltpu.CompilerParams(collective_id=0, has_side_effects=True, vmem_limit_bytes=56 * 2**20),
        name="influence",
    )(activations.reshape(flat), out_grads.reshape(flat), proj_in.T, proj_out.T, fisher_inv, grad_store)
    return result.reshape(per, out_rows // per, examples).transpose(1, 0, 2).reshape(out_rows, examples)


def solution(mesh):
    placed = (
        P("store", None, "width"),
        P("store", None, "width"),
        P("width", None),
        P("width", None),
        P("store", "width"),
        P("store", "width"),
    )
    return jax.shard_map(
        functools.partial(body, mesh.shape["width"], mesh.shape["store"]),
        mesh=mesh, in_specs=placed, out_specs=P("width", "store"), check_vma=False,
    )
```

time: 209 us -> 59.3 us (0.28)
  waiting for transfers between devices: 149 us -> 0 us
  Pallas kernels: 0 us -> 57.4 us
  matrix products: 33.2 us -> 0 us
  between operations: 13.1 us -> 0.01 us
  blocking collectives: 11.2 us -> 0 us
    psum x2 -> x0, waiting for transfers between devices: 125 us -> none  [the longest x1 72.5 us: body(): summed = lax.psum(paired, 'width')]
    pallas_call x0 -> x1, Pallas kernels: none -> 57.4 us  [body(): pl.pallas_call(functools.partial(kernel, (wide, stores, per, seq, rank)),...]
    dot_general x5 -> x0, matrix products: 33.2 us -> none  [the longest x1 12.2 us: body(): jnp.dot(precond, grad_store.T, precision=lax.Precision.HIGHEST)]
    reduce_scatter x1 -> x0, waiting for transfers between devices: 23.9 us -> none  [body(): lax.psum_scatter(jnp.dot(precond, grad_store.T, precision=lax.Precision.H...]
    all_to_all x1 -> x0, blocking collectives: 11.2 us -> none  [body(): lax.all_to_all(gradient, 'store', split_axis=1, concat_axis=0, tiled=True)]
  transfers between devices with their start and end apart: 3 -> 0, of which waited for: 3 -> 0; matrix products, arithmetic and copies ran while one was open for 0% -> 0% of each run, Pallas kernels for 0% -> 0%
where the time goes in v2:
time: 59.3 us; the launch traced here: 59.2 us
  Pallas kernels  57.4 us (97%)
  local copies, waits for them, and re-layouts  1.75 us (3%)
    pallas_call x1, Pallas kernels, body(): pl.pallas_call(functools.partial(kernel, (wide, stores, per, seq, rank)),...  57.4 us

profile of v2, /device:TPU:0, one launch (start us, length us, event | category | flops | bytes accessed | tf_op | source)
XLA Modules:
  0.0 59.2 jit_solution(13344265645657934387)
XLA Ops:
  0.0 57.4 %influence.1 = f32[16,2048]{1,0:T(8,128)} custom-call(bf16[4096,2048]{1,0:T(8,128)(2,1)} %bitcast.7, bf16[4096,2048]{1,0:T(8,128)(2,1)} %bitcast.8, bf16[64,2048]{1,0:T(8,128)(2,1)} %bitcast.10, bf16[64,2048]{1,0:T(8,128)(2,1)} %bitcast.11, f32[512,1024]{1,0:T(8,128)} %fis.1, f32[2048,1024]{1,0:T(8,128)} %sto.1), custom_call_target="tpu_custom_call" | custom-call | tf_op jit(solution)/shard_map/influence/pallas_call | solution.py:315
  57.4 1.0 %copy.7 = f32[8,2,2048]{2,1,0:T(2,128)S(1)} copy(f32[8,2,2048]{2,0,1:T(8,128)} %bitcast.9) | data formatting | bytes 262144 | tf_op jit(solution)/shard_map/transpose | solution.py:364
  58.4 0.7 %reshape.15 = f32[16,2048]{1,0:T(8,128)} reshape(f32[8,2,2048]{2,1,0:T(2,128)S(1)} %copy.7) | data formatting | bytes 262144 | tf_op jit(solution)/shard_map/reshape | solution.py:364

commit v3 on v2

--- a/solution.py
+++ b/solution.py
@@ -245,23 +245,23 @@
 
         lax.fori_loop(0, 16, part, 0)
 
-    for p in range(per):
-        if p == per - 1:
-            load_f.start()
-        lax.fori_loop(p * each, (p + 1) * each, project, 0)
-        if p + 1 < per:
-            forward(p)
+    late = (per - 1) * each + n1
+    lax.fori_loop(0, late, project, 0)
+    load_f.start()
+    for p in range(per - 1):
+        forward(p)
+    lax.fori_loop(late, per * each, project, 0)
     load_s.start()
     split_fisher()
     if per == 2:
+        forward(1)
         gradient(0)
+        split_store()
         gather(0)
-        forward(1)
+        gradient(1)
         condition(0)
-        split_store()
-        gradient(1)
+        gather(1)
         combine(0)
-        gather(1)
         condition(1)
         score(0)
         combine(1)

time: 59.3 us -> 64.9 us (1.094)
  Pallas kernels: 57.4 us -> 63 us
    pallas_call x1, Pallas kernels: 57.4 us -> 63 us  [body(): pl.pallas_call(functools.partial(kernel, (wide, stores, per, seq, rank)),...]
where the time goes in v3:
time: 64.9 us; the launch traced here: 64.7 us
  Pallas kernels  63 us (97%)
  local copies, waits for them, and re-layouts  1.75 us (3%)
    pallas_call x1, Pallas kernels, body(): pl.pallas_call(functools.partial(kernel, (wide, stores, per, seq, rank)),...  63 us

profile of v3, /device:TPU:0, one launch (start us, length us, event | category | flops | bytes accessed | tf_op | source)
XLA Modules:
  0.0 64.7 jit_solution(13017947326850539337)
XLA Ops:
  0.0 63.0 %influence.1 = f32[16,2048]{1,0:T(8,128)} custom-call(bf16[4096,2048]{1,0:T(8,128)(2,1)} %bitcast.7, bf16[4096,2048]{1,0:T(8,128)(2,1)} %bitcast.8, bf16[64,2048]{1,0:T(8,128)(2,1)} %bitcast.10, bf16[64,2048]{1,0:T(8,128)(2,1)} %bitcast.11, f32[512,1024]{1,0:T(8,128)} %fis.1, f32[2048,1024]{1,0:T(8,128)} %sto.1), custom_call_target="tpu_custom_call" | custom-call | tf_op jit(solution)/shard_map/influence/pallas_call | solution.py:315
  63.0 1.0 %copy.7 = f32[8,2,2048]{2,1,0:T(2,128)S(1)} copy(f32[8,2,2048]{2,0,1:T(8,128)} %bitcast.9) | data formatting | bytes 262144 | tf_op jit(solution)/shard_map/transpose | solution.py:364
  64.0 0.7 %reshape.15 = f32[16,2048]{1,0:T(8,128)} reshape(f32[8,2,2048]{2,1,0:T(2,128)S(1)} %copy.7) | data formatting | bytes 262144 | tf_op jit(solution)/shard_map/reshape | solution.py:364

commit v4 on v2

--- a/solution.py
+++ b/solution.py
@@ -204,12 +204,12 @@
         peer = (w + d) % wide
         return remote(scb.at[p, c, peer], rsc.at[p, c, d], sc.at[p, c, d], rc.at[p, c, d], "width", peer)
 
-    def score(p):
-        for d in range(1, stores):
+    def score(p, first, stop):
+        for d in range(1, stores if first == 0 else 1):
             ship_g(p, d).wait_recv()
         precond = jnp.concatenate([pfull[p, r] for r in range(stores)], axis=0 if by_rows else 1)
         stacked = jnp.concatenate(split(precond), axis=0)
-        for c in range(COLS):
+        for c in range(first, stop):
             rows = pl.ds(c * span, span)
             double = dot(shi[rows, :], stacked, ((1,), (1,))) + dot(slo[rows, :], stacked, ((1,), (1,)))
             double = double.T
@@ -225,7 +225,9 @@
             for d in range(1, wide):
                 ship_c(p, c, d).wait_recv()
                 total = total + rsc[p, c, d]
-            out[p * stores : (p + 1) * stores, c * span : (c + 1) * span] = total
+            for i in range(stores):
+                row = i * per + p
+                out[row : row + 1, c * span : (c + 1) * span] = total[i : i + 1]
 
     load_f = pltpu.make_async_copy(fis, fraw, lsem.at[0])
     load_s = pltpu.make_async_copy(sto, sraw, lsem.at[1])
@@ -263,9 +265,10 @@
         combine(0)
         gather(1)
         condition(1)
-        score(0)
+        score(0, 0, COLS // 2)
         combine(1)
-        score(1)
+        score(0, COLS // 2, COLS)
+        score(1, 0, COLS)
     else:
         forward(per - 1)
         split_store()
@@ -274,7 +277,7 @@
             gather(p)
             condition(p)
             combine(p)
-            score(p)
+            score(p, 0, COLS)
     for p in range(per):
         finish(p)
 
@@ -312,7 +315,7 @@
     span = examples // COLS
     dma = pltpu.SemaphoreType.DMA
     flat = (group * seq, width)
-    result = pl.pallas_call(
+    return pl.pallas_call(
         functools.partial(kernel, (wide, stores, per, seq, rank)),
         out_shape=jax.ShapeDtypeStruct((out_rows, examples), F32),
         in_specs=[pl.BlockSpec(memory_space=pl.ANY)] * 2
@@ -361,7 +364,6 @@
         compiler_params=pltpu.CompilerParams(collective_id=0, has_side_effects=True, vmem_limit_bytes=56 * 2**20),
         name="influence",
     )(activations.reshape(flat), out_grads.reshape(flat), proj_in.T, proj_out.T, fisher_inv, grad_store)
-    return result.reshape(per, out_rows // per, examples).transpose(1, 0, 2).reshape(out_rows, examples)
 
 
 def solution(mesh):

time: 59.3 us -> 58.9 us (level)
    unnamed x0 -> x1, local copies, waits for them, and re-layouts: none -> 1.57 us
    transpose x1 -> x0, local copies, waits for them, and re-layouts: 1.01 us -> none  [body(): result.reshape(per, out_rows // per, examples).transpose(1, 0, 2)]
    reshape x1 -> x0, local copies, waits for them, and re-layouts: 0.75 us -> none  [body(): result.reshape(per, out_rows // per, examples).transpose(1, 0, 2)]
where the time goes in v4:
time: 58.9 us; the launch traced here: 58.8 us
  Pallas kernels  57.2 us (97%)
  local copies, waits for them, and re-layouts  1.57 us (3%)
    pallas_call x1, Pallas kernels, body(): pl.pallas_call(functools.partial(kernel, (wide, stores, per, seq, rank)),...  57.2 us
    unnamed x1, local copies, waits for them, and re-layouts  1.57 us

profile of v4, /device:TPU:0, one launch (start us, length us, event | category | flops | bytes accessed | tf_op | source)
XLA Modules:
  0.0 58.8 jit_solution(2079969167869254444)
XLA Ops:
  0.0 57.2 %influence.1 = f32[16,2048]{1,0:T(8,128)} custom-call(bf16[4096,2048]{1,0:T(8,128)(2,1)} %bitcast.4, bf16[4096,2048]{1,0:T(8,128)(2,1)} %bitcast.5, bf16[64,2048]{1,0:T(8,128)(2,1)} %bitcast.6, bf16[64,2048]{1,0:T(8,128)(2,1)} %bitcast.7, f32[512,1024]{1,0:T(8,128)} %fis.1, f32[2048,1024]{1,0:T(8,128)} %sto.1), custom_call_target="tpu_custom_call" | custom-call | tf_op jit(solution)/shard_map/influence/pallas_call | solution.py:318
  57.2 1.6 %copy.8 = f32[16,2048]{1,0:T(8,128)} copy(f32[16,2048]{1,0:T(8,128)} %influence.1) | data formatting | bytes 262144
